TPU v7x, 256 devices: a whole 4x4x8 slice. The times are simulated.
256 devices in a mesh: dp: 16 (over y_lo, z), factor: 16 (over x, y_hi, core).
Axes of the slice: x: 4, y: 4 (y_hi: 2, y_lo: 2; y = y_hi * 2 + y_lo), z: 8, core: 2. Of those that a mesh axis runs over, the one named last changes fastest.
Arguments:
- train_inputs: bfloat16 [128, 8, 64, 320], P('dp'), may hold values from -6 to 6
- train_cotangents: bfloat16 [128, 8, 64, 320], P('dp'), may hold values from -0.26367188 to 0.26367188
- query_inputs: bfloat16 [16, 8, 64, 320], P('dp'), may hold values from -6 to 6
- query_cotangents: bfloat16 [16, 8, 64, 320], P('dp'), may hold values from -0.26367188 to 0.26367188
- timesteps: int32 [128], P('dp'), may hold values from 0 to 999
- input_basis: bfloat16 [2880, 2880], P('dp', 'factor'), may hold values from -0.109375 to 0.109375
- output_basis: bfloat16 [320, 320], replicated, may hold values from -0.3125 to 0.3125
- eigenvalues: float32 [320, 2880], P(None, 'factor'), may hold values from 0.1 to 10
Outputs:
- scores: float32 [128], P('dp')
- query_proj: float32 [320, 2880], P(None, 'factor')
All inputs are finite; a program needn't handle non-finite values.
Results may differ from a plain program's by a relative error of at most 0.0037.
Values may be sent and summed in bfloat16 or wider, within the bound.
A program may use at most 192 MiB of HBM per device.

v0:
```python
import math

import jax
import jax.numpy as jnp
from jax import lax
from jax.sharding import PartitionSpec as P

damping = 0.01


def patch_matrix(activations):
    batch, rows_count, cols_count, channels = activations.shape
    padded = jnp.pad(activations, ((0, 0), (1, 1), (1, 1), (0, 0)))
    taps = [
        padded[:, row_off : row_off + rows_count, col_off : col_off + cols_count, :]
        for row_off in range(3)
        for col_off in range(3)
    ]
    return jnp.concatenate(taps, axis=-1).reshape(batch * rows_count * cols_count, 9 * channels)


def on_device(
    train_inputs,
    train_cotangents,
    query_inputs,
    query_cotangents,
    timesteps,
    input_basis,
    output_basis,
    eigenvalues,
):
    high = lax.Precision.HIGHEST
    channels = output_basis.shape[0]
    width = input_basis.shape[0] * lax.axis_size("dp")
    batch = train_inputs.shape[0]
    positions = train_inputs.shape[1] * train_inputs.shape[2]
    panel_width = input_basis.shape[1]
    train_patches = patch_matrix(train_inputs)
    query_patches = patch_matrix(query_inputs)
    query_flat = query_cotangents.reshape(-1, channels)
    partial_query = jnp.dot(query_flat.T, query_patches, preferred_element_type=jnp.float32)
    count = query_inputs.shape[0] * lax.axis_size("dp")
    query_grad = lax.psum(partial_query, "dp") / count
    piece = lax.all_gather(input_basis, "dp", axis=0, tiled=True)
    query_part = jnp.dot(query_grad, piece.astype(jnp.float32), precision=high)
    projected = jnp.dot(train_patches, piece, preferred_element_type=jnp.float32)
    basis_out = output_basis.astype(jnp.float32)
    query_proj = jnp.dot(basis_out.T, query_part, precision=high) / (eigenvalues + damping)
    rotated = jnp.dot(
        train_cotangents.reshape(-1, channels), output_basis, preferred_element_type=jnp.float32
    )
    rotated = rotated.astype(jnp.bfloat16).reshape(batch, positions, channels)
    projected = projected.astype(jnp.bfloat16).reshape(batch, positions, panel_width)
    train_proj = jnp.einsum("bpc,bpk->bck", rotated, projected, preferred_element_type=jnp.float32)
    partial_scores = jnp.einsum("bck,ck->b", train_proj, query_proj, precision=high)
    raw_scores = lax.psum(partial_scores, "factor")
    phase = (timesteps.astype(jnp.float32) / 1000.0 + 0.008) / 1.008 * (math.pi / 2)
    weight = jnp.sin(phase)
    scores = raw_scores * weight / math.sqrt(channels * width)
    return (scores, query_proj)


def solution(mesh):
    in_specs = (
        P("dp", None, None, None),
        P("dp", None, None, None),
        P("dp", None, None, None),
        P("dp", None, None, None),
        P("dp"),
        P("dp", "factor"),
        P(),
        P(None, "factor"),
    )
    out_specs = (P("dp"), P(None, "factor"))
    return jax.shard_map(
        on_device, mesh=mesh, in_specs=in_specs, out_specs=out_specs, check_vma=False
    )
```

profile of v0, /device:TPU:1, one launch (start us, length us, event | category | flops | bytes accessed | tf_op | source)
XLA Modules:
  0.0 234.6 jit_solution(13893424670948783343)
XLA Ops:
  7.2 0.0 copy-start
  7.2 0.0 all-reduce.4.cloned.1.call-start
  7.2 4.6 %pad_slice_fusion.8 = (bf16[1,8,64,320]{3,2,1,0:T(8,128)(2,1)}, bf16[1,8,64,320]{3,2,1,0:T(8,128)(2,1)}, bf16[1,8,64,320]{3,2,1,0:T(8,128)(2,1)}, bf16[1,8,64,32...) fusion(bf16[1,8,64,320]{3,2,1,0:T(8,128)(2,1)} %param.10), kind=kLoop, calls=%fused_computation.25 | loop fusion | bytes 2949120 | tf_op jit(solution)/shard_map/slice | solution.py:15
  11.9 6.2 %concatenate.7 = bf16[1,8,64,2880]{3,2,1,0:T(8,128)(2,1)} concatenate(bf16[1,8,64,320]{3,2,1,0:T(8,128)(2,1)} %get-tuple-element.17, bf16[1,8,64,320]{3,2,1,0:T(8,128)(2,1)} %get-tuple-element.11, bf16[1,8,64,320]{3,2,1,0:T(8,128)(2,1)} %get-tuple-element.12, bf16[1,8,64,320]{3,2,1,0:T(8,128)(2,1)} %get-tuple-element.13, bf16[1,8,64,320]{3,2,1,0:T(8,128)(2,1)S(1)} %copy-done.2, ...), dimensions={3} | concatenate | bytes 5898240 | tf_op jit(solution)/shard_map/concatenate | solution.py:19
  18.0 5.1 %convolution_bitcast_fusion = f32[320,2880]{1,0:T(8,128)} fusion(bf16[1,8,64,2880]{3,2,1,0:T(8,128)(2,1)} %concatenate.7, bf16[1,8,64,320]{3,2,1,0:T(8,128)(2,1)} %param.11), kind=kOutput, calls=%fused_computation.10 | convolution fusion | flops 943718400 | bytes 6963200 | tf_op jit(solution)/shard_map/dot_general | solution.py:41
  23.1 0.0 all-reduce.4.cloned.1.call-update
  23.1 0.9 copy-done.6
  24.0 52.8 %all-gather = bf16[16,180,180]{2,1,0:T(8,128)(2,1)} all-gather(bf16[1,180,180]{2,1,0:T(8,128)(2,1)S(1)} %bitcast.43), channel_id=1, replica_groups=mesh['dp'=16,'factor'=16] {'dp'}, dimensions={0}, use_global_device_ids=true | all-gather | bytes 1101600 | tf_op jit(solution)/shard_map/all_gather | solution.py:44
  76.8 3.5 %reshape.35 = bf16[2880,180]{1,0:T(8,128)(2,1)} reshape(bf16[16,180,180]{2,1,0:T(8,128)(2,1)} %all-gather) | data formatting | bytes 2073600
  80.3 20.4 %pad_slice_fusion = (bf16[8,8,64,320]{3,2,1,0:T(8,128)(2,1)}, bf16[8,8,64,320]{3,2,1,0:T(8,128)(2,1)}, bf16[8,8,64,320]{3,2,1,0:T(8,128)(2,1)}, bf16[8,8,64,320]...) fusion(bf16[8,8,64,320]{3,2,1,0:T(8,128)(2,1)} %param.8), kind=kLoop, calls=%fused_computation.1 | loop fusion | bytes 23592960 | tf_op jit(solution)/shard_map/slice | solution.py:15
  100.7 37.5 %concatenate.6 = bf16[8,8,64,2880]{3,2,1,0:T(8,128)(2,1)} concatenate(bf16[8,8,64,320]{3,2,1,0:T(8,128)(2,1)} %get-tuple-element.9, bf16[8,8,64,320]{3,2,1,0:T(8,128)(2,1)} %get-tuple-element.3, bf16[8,8,64,320]{3,2,1,0:T(8,128)(2,1)} %get-tuple-element.4, bf16[8,8,64,320]{3,2,1,0:T(8,128)(2,1)} %get-tuple-element.5, bf16[8,8,64,320]{3,2,1,0:T(8,128)(2,1)} %param.8, ...), dimensions={3} | concatenate | bytes 47185920 | tf_op jit(solution)/shard_map/concatenate | solution.py:19
  138.2 14.1 %convolution_convert_fusion.1 = bf16[4096,180]{0,1:T(8,128)(2,1)} fusion(bf16[4096,2880]{1,0:T(8,128)(2,1)} %bitcast.38, bf16[2880,180]{1,0:T(8,128)(2,1)} %reshape.35), kind=kOutput, calls=%fused_computation.9 | convolution fusion | flops 4247470080 | bytes 26104320 | tf_op jit(solution)/shard_map/dot_general | solution.py:46
  152.3 2.1 copy.18
  154.3 0.1 slice_bitcast_fusion
  154.5 1.6 convolution_convert_fusion
  156.0 2.7 %fusion.3 = f32[8,320,180]{1,2,0:T(8,128)} fusion(bf16[40,8,8,512]{3,2,1,0:T(8,128)(2,1)S(1)} %bitcast.39, bf16[8,512,180]{1,0,2:T(8,128)(2,1)S(1)} %slice_bitcast_fusion), kind=kOutput, calls=%fused_computation.14 | convolution fusion | flops 471859200 | bytes 5939200 | tf_op jit(solution)/shard_map/bpc,bpk->bck/dot_general | solution.py:54
  158.8 15.3 %all-reduce.4.cloned.1.call-done = f32[320,2880]{1,0:T(8,128)} async-done(((f32[320,2880]{1,0:T(8,128)}), f32[320,2880]{1,0:T(8,128)}) %all-reduce.4.cloned.1.call-update) | async-done | bytes 3686416 | tf_op jit(solution)/shard_map/psum | solution.py:43
  174.1 5.4 %fusion = f32[320,180]{0,1:T(8,128)S(1)} fusion(bf16[2880,180]{1,0:T(8,128)(2,1)} %reshape.35, f32[320,2880]{1,0:T(8,128)} %all-reduce.4.cloned.1.call-done), kind=kOutput, calls=%fused_computation.11 | convolution fusion | flops 1991577600 | bytes 4953600 | tf_op jit(solution)/shard_map/dot_general | solution.py:45
  179.4 0.0 copy-start.8
  179.5 0.5 fusion.10
  179.9 0.0 copy-start.3
  180.0 4.9 %fusion.11 = f32[8]{0:T(128)S(1)} fusion(f32[8,320,180]{1,2,0:T(8,128)S(1)} %copy-done.1, f32[320,180,1]{0,1,2:T(8,128)S(1)} %bitcast.42), kind=kOutput, calls=%fused_computation.24 | convolution fusion | flops 5529600 | bytes 2073632 | tf_op jit(solution)/shard_map/bck,ck->b/dot_general | solution.py:55
  184.8 42.3 %psum.15 = f32[8]{0:T(128)S(1)} all-reduce(f32[8]{0:T(128)S(1)} %fusion.11), channel_id=1, replica_groups=mesh['dp'=16,'factor'=16] {'factor'}, use_global_device_ids=true, to_apply=%region_1.2 | all-reduce | flops 8 | bytes 64 | tf_op jit(solution)/shard_map/psum | solution.py:56
  227.2 0.6 multiply_multiply_fusion
  (14 shorter events, 0.0 us)
Async XLA Ops:
  7.2 147.3 %copy-start = (bf16[8,8,64,320]{3,2,1,0:T(8,128)(2,1)S(1)}, bf16[8,8,64,320]{3,2,1,0:T(8,128)(2,1)}, u32[]{:S(2)}) copy-start(bf16[8,8,64,320]{3,2,1,0:T(8,128)(2,1)} %param.9) | copy-start | bytes 7864324
  7.2 4.7 %copy-start.2 = (bf16[1,8,64,320]{3,2,1,0:T(8,128)(2,1)S(1)}, bf16[1,8,64,320]{3,2,1,0:T(8,128)(2,1)}, u32[]{:S(2)}) copy-start(bf16[1,8,64,320]{3,2,1,0:T(8,128)(2,1)} %param.10) | copy-start | bytes 983044
  7.2 166.9 %all-reduce.4.cloned.1.call-start = ((), (), s32[]{:S(2)}) async-start(), calls=%async_computation | async-start | bytes 7536640 | tf_op jit(solution)/shard_map/psum | solution.py:43
  23.1 0.9 copy-start.6
  152.3 2.2 copy-start.4
  174.1 5.4 %copy-start.5 = (bf16[320,320]{1,0:T(8,128)(2,1)S(1)}, bf16[320,320]{1,0:T(8,128)(2,1)}, u32[]{:S(2)}) copy-start(bf16[320,320]{1,0:T(8,128)(2,1)} %param.14) | copy-start | bytes 614404
  174.1 5.4 %copy-start.7 = (f32[320,180]{0,1:T(8,128)S(1)}, f32[320,180]{0,1:T(8,128)}, u32[]{:S(2)}) copy-start(f32[320,180]{0,1:T(8,128)} %param.15) | copy-start | bytes 691204
  174.1 5.9 %copy-start.1 = (f32[8,320,180]{1,2,0:T(8,128)S(1)}, f32[8,320,180]{1,2,0:T(8,128)}, u32[]{:S(2)}) copy-start(f32[8,320,180]{1,2,0:T(8,128)} %fusion.3) | copy-start | bytes 5529604
  179.4 47.7 %copy-start.8 = (s32[8]{0:T(128)S(1)}, s32[8]{0:T(128)}, u32[]{:S(2)}) copy-start(s32[8]{0:T(128)} %param.12) | copy-start | bytes 100
  179.9 47.8 %copy-start.3 = (f32[320,180]{0,1:T(8,128)}, f32[320,180]{0,1:T(8,128)S(1)}, u32[]{:S(2)}) copy-start(f32[320,180]{0,1:T(8,128)S(1)} %fusion.10) | copy-start | bytes 691204
Sparse Core Ops, SparseCore 0:
  23.2 150.7 all-reduce.3
where the time goes:
time: 238 us; the launch traced here: 235 us
  blocking collectives  95.1 us (40%)
  local copies, waits for them, and re-layouts  75.3 us (32%)
  matrix products  34.2 us (14%)
  waiting for transfers between devices  15.3 us (6%)
  between operations  14.1 us (6%)
    all_gather x1, blocking collectives, on_device(): piece = lax.all_gather(input_basis, 'dp', axis=0, tiled=True)  52.8 us
    concatenate x2, local copies, waits for them, and re-layouts, patch_matrix(): jnp.concatenate(taps, axis=-1)  43.6 us
    psum x1, blocking collectives, on_device(): raw_scores = lax.psum(partial_scores, 'factor')  42.3 us
    slice x2, local copies, waits for them, and re-layouts, patch_matrix(): padded[:, row_off:row_off + rows_count, col_off:col_off + cols_count, :]  25.1 us
    psum x1, waiting for transfers between devices, on_device(): query_grad = lax.psum(partial_query, 'dp') / count  15.3 us
    dot_general x1, matrix products, on_device(): jnp.dot(train_patches, piece, preferred_element_type=jnp.float32)  14.1 us
    unnamed x20, local copies, waits for them, and re-layouts  6.49 us
    dot_general x1, matrix products, on_device(): query_part = jnp.dot(query_grad, piece.astype(jnp.float32), precision=high)  5.35 us
  transfers between devices with their start and end apart: 1, of which 1 were waited for; matrix products, arithmetic and copies ran while one was open for 35% of the time, Pallas kernels for 0%

commit v1 on v0

v1 whole, which is shorter than its diff:
```python
import functools
import math

import jax
import jax.numpy as jnp
from jax import lax
from jax.experimental import pallas as pl
from jax.experimental.pallas import tpu as pltpu
from jax.sharding import PartitionSpec as P

damping = 0.01
MESH = pl.DeviceIdType.MESH
bf16 = jnp.bfloat16
f32 = jnp.float32

NY, NZ = 2, 8
ND, NF = 16, 16
CH = 320
SIDE = 180
CS = 40
BLOCKS = 13
POS = 512
BATCH = 8
PREPARED = 5
PACK = 288

WHOLE, HALF_A, HALF_B = (0, 288), (0, 144), (144, 144)


def norm(origin):
    return (origin[0] % NY, origin[1] % NZ)


START = [
    ((0, 0), WHOLE, (0, 2)), ((0, 0), WHOLE, (0, -2)),
    ((0, 0), WHOLE, (0, 1)), ((0, 0), WHOLE, (0, -1)),
    ((0, 0), WHOLE, (1, 0)),
]
COLUMN = [
    ((0, -2), HALF_A, (0, 2)), ((0, 2), HALF_B, (0, -2)),
    ((0, -2), WHOLE, (0, 1)), ((0, 2), WHOLE, (0, -1)),
]
ACROSS_NEAR = [((0, k), WHOLE, (1, 0)) for k in (1, -1, 2, -2)]
ACROSS_FAR = [((0, k), WHOLE, (1, 0)) for k in (3, -3, 4)]
PLAN = START + COLUMN + ACROSS_NEAR + ACROSS_FAR
LANDS = {}
for number, (origin, rows, hop) in enumerate(PLAN):
    place = (norm((origin[0] - hop[0], origin[1] - hop[1])), rows)
    assert place not in LANDS
    LANDS[place] = number


DP_STEPS = sorted(
    ((dy, dz) for dy in range(NY) for dz in range(NZ) if dy or dz),
    key=lambda step: -(step[0] + min(step[1], NZ - step[1])),
)
FACTOR_STEPS = sorted(
    ((dx, dh, dc) for dx in range(4) for dh in range(2) for dc in range(2) if dx or dh or dc),
    key=lambda step: -(min(step[0], 4 - step[0]) + 2 * step[1] + 0.1 * step[2]),
)


def block_of(y, part):
    return jnp.where(part < BLOCKS - 1, part + 11 * y, 14 + 9 * y)


def fill_patches(raw, xl, slot):
    x = raw.reshape(POS, CH).astype(f32)
    col = lax.broadcasted_iota(jnp.int32, (POS, 1), 0) % 64
    main, rest = x[:, :256], x[:, 256:]
    zero_rest = jnp.zeros((POS, 64), f32)

    def left(v):
        return jnp.where(col == 0, 0.0, pltpu.roll(v, 1, 0))

    def right(v):
        return jnp.where(col == 63, 0.0, pltpu.roll(v, POS - 1, 0))

    wide = jnp.concatenate([rest, zero_rest], axis=1)
    swapped = pltpu.roll(wide, 64, 1)
    inside = pl.ds(64, POS)
    xl[slot, inside, 0:256] = left(main).astype(bf16)
    xl[slot, inside, 256:512] = main.astype(bf16)
    xl[slot, inside, 512:768] = right(main).astype(bf16)
    xl[slot, inside, 768:896] = (left(wide) + swapped).astype(bf16)
    xl[slot, inside, 896:1024] = right(wide).astype(bf16)


def kernel(
    x_hbm, cot_hbm, qx_hbm, qcot_hbm, bin_hbm, bout_hbm, eig_hbm, time_ref,
    score_ref, proj_hbm,
    x_raw, cot_raw, qx_raw, qcot_raw, bin_raw, bout, bout_t, eig_raw, scale,
    panels, flat, panel, xl, r_all, acc, w_all, proj_out,
    mq, p1_src, p1_dst, p2_buf, m_stack, ag_buf, v_flat, q_pad, ar_buf,
    load_sem, x_sem, cot_sem,
    bin_send, bin_recv, p1_send, p1_recv, p2_send, p2_recv, ag_send, ag_recv, ar_send, ar_recv,
):
    d = lax.axis_index("dp")
    f = lax.axis_index("factor")
    y, z = d // NZ, d % NZ
    fx, fh, fc = f // 4, f // 2 % 2, f % 2

    def dp_at(k, sign=1):
        dy, dz = DP_STEPS[k]
        return (y + dy) % NY * NZ + (z + sign * dz + NZ) % NZ

    def factor_at(k, sign=1):
        dx, dh, dc = FACTOR_STEPS[k]
        return (fx + sign * dx + 4) % 4 * 4 + (fh + dh) % 2 * 2 + (fc + dc) % 2

    bin_load = pltpu.make_async_copy(bin_hbm, bin_raw, load_sem.at[0])
    qx_load = pltpu.make_async_copy(qx_hbm.at[0], qx_raw, load_sem.at[1])
    qcot_load = pltpu.make_async_copy(qcot_hbm.at[0], qcot_raw, load_sem.at[2])
    bout_load = pltpu.make_async_copy(bout_hbm, bout, load_sem.at[3])
    eig_load = pltpu.make_async_copy(eig_hbm, eig_raw, load_sem.at[4])

    def x_load(b):
        return pltpu.make_async_copy(x_hbm.at[b], x_raw.at[b], x_sem.at[b])

    def cot_load(b):
        return pltpu.make_async_copy(cot_hbm.at[b], cot_raw.at[b], cot_sem.at[b])

    for copy in (bin_load, qx_load, qcot_load, bout_load, eig_load):
        copy.start()

    barrier = pltpu.get_barrier_semaphore()
    for k in range(ND - 1):
        pl.semaphore_signal(barrier, inc=1, device_id=(dp_at(k), f), device_id_type=MESH)
    for k in range(NF - 1):
        pl.semaphore_signal(barrier, inc=1, device_id=(d, factor_at(k)), device_id_type=MESH)
    for b in range(BATCH):
        x_load(b).start()
        cot_load(b).start()

    xl[BATCH, 0:64, :] = jnp.zeros((64, 1024), bf16)
    xl[BATCH, 576:640, :] = jnp.zeros((64, 1024), bf16)

    bin_load.wait()
    block = bin_raw[...].astype(f32)
    tail_a = block[0:96, 128:180]
    tail_b = jnp.concatenate([block[96:180, 128:180], jnp.zeros((12, 52), f32)], axis=0)
    gap = jnp.zeros((96, 12), f32)
    panels[pl.ds(d, 1), 0:192, :] = jnp.concatenate(
        [block[:, 0:128], jnp.zeros((12, 128), f32)], axis=0
    ).astype(bf16)[None]
    panels[pl.ds(d, 1), 192:288, :] = jnp.concatenate([tail_a, gap, tail_b, gap], axis=1).astype(bf16)[None]

    qx_load.wait()
    qcot_load.wait()
    fill_patches(qx_raw[...], xl, BATCH)
    query_t = qcot_raw[...].reshape(POS, CH).T
    for half in range(NY):
        number = block_of(half, jnp.minimum(f, BLOCKS - 1))
        mq[half] = jnp.dot(
            query_t,
            xl[
                BATCH,
                pl.ds(pl.multiple_of(number // 8 * 64, 64), POS),
                pl.ds(pl.multiple_of(number % 8 * 128, 128), 128),
            ],
            preferred_element_type=f32,
        )
    for part in range(ND):
        row = part % NZ * CS
        p1_src[part] = mq[part // NZ, row : row + CS, :].astype(bf16)

    def basis_copy(number):
        origin, (start, count), hop = PLAN[number]
        slot = (y + origin[0]) % NY * NZ + (z + origin[1] + NZ) % NZ
        view = panels.at[slot, pl.ds(start, count)]
        peer = (y + hop[0]) % NY * NZ + (z + hop[1] + NZ) % NZ
        return pltpu.make_async_remote_copy(
            src_ref=view, dst_ref=view, send_sem=bin_send.at[number], recv_sem=bin_recv.at[number],
            device_id=(peer, f), device_id_type=MESH,
        )

    seen = set()

    def basis_wait(origin):
        for place, number in LANDS.items():
            if place[0] != norm(origin) or place in seen:
                continue
            seen.add(place)
            start, count = place[1]
            slot = (y + place[0][0]) % NY * NZ + (z + place[0][1]) % NZ
            view = panels.at[slot, pl.ds(start, count)]
            pltpu.make_async_remote_copy(
                src_ref=view, dst_ref=view, send_sem=bin_send.at[number], recv_sem=bin_recv.at[number],
                device_id=(d, f), device_id_type=MESH,
            ).wait_recv()

    def basis_forward(copies):
        for copy in copies:
            basis_wait(copy[0])
            basis_copy(PLAN.index(copy)).start()

    def to_dp(k, src, dst, send, recv):
        return pltpu.make_async_remote_copy(
            src_ref=src, dst_ref=dst, send_sem=send.at[k], recv_sem=recv.at[k],
            device_id=(dp_at(k), f), device_id_type=MESH,
        )

    def to_factor(k, src, dst, send, recv):
        return pltpu.make_async_remote_copy(
            src_ref=src, dst_ref=dst, send_sem=send.at[k], recv_sem=recv.at[k],
            device_id=(d, factor_at(k)), device_id_type=MESH,
        )

    def p1_copy(k):
        return to_dp(k, p1_src.at[dp_at(k)], p1_dst.at[d], p1_send, p1_recv)

    def p1_land(k):
        sender = dp_at(k, -1)
        return to_dp(k, p1_src.at[sender], p1_dst.at[sender], p1_send, p1_recv)

    def p2_copy(k):
        return to_factor(k, p2_buf.at[f], p2_buf.at[f], p2_send, p2_recv)

    def p2_land(k):
        sender = factor_at(k, -1)
        return sender, to_factor(k, p2_buf.at[sender], p2_buf.at[sender], p2_send, p2_recv)

    def ag_copy(k):
        return to_dp(k, ag_buf.at[d], ag_buf.at[d], ag_send, ag_recv)

    def ag_land(k):
        sender = dp_at(k, -1)
        return to_dp(k, ag_buf.at[sender], ag_buf.at[sender], ag_send, ag_recv)

    def ar_copy(k):
        return to_factor(k, ar_buf.at[f], ar_buf.at[f], ar_send, ar_recv)

    def ar_land(k):
        sender = factor_at(k, -1)
        return to_factor(k, ar_buf.at[sender], ar_buf.at[sender], ar_send, ar_recv)

    pl.semaphore_wait(barrier, ND + NF - 2)

    @pl.when(f < BLOCKS)
    def _():
        for k in range(ND - 1):
            p1_copy(k).start()

    for number in range(len(START)):
        basis_copy(number).start()

    p1_dst[pl.ds(d, 1)] = p1_src[pl.ds(d, 1)]

    flat[:, 128:256] = jnp.zeros((9 * CH, 128), f32)
    panel[...] = jnp.zeros_like(panel)
    q_pad[...] = jnp.zeros_like(q_pad)
    bout_load.wait()
    bout_t[...] = bout[...].T
    eig_load.wait()
    scale[...] = (1.0 / 16) / (eig_raw[...].T + damping)

    def prepare(b, carry):
        x_load(b).wait()
        cot_load(b).wait()
        xl[b, 0:64, :] = jnp.zeros((64, 1024), bf16)
        xl[b, 576:640, :] = jnp.zeros((64, 1024), bf16)
        fill_patches(x_raw[b], xl, b)
        rotated_cot = jnp.dot(cot_raw[b].reshape(POS, CH), bout[...], preferred_element_type=f32)
        r_all[b] = rotated_cot.astype(bf16).T
        return carry

    lax.fori_loop(0, PREPARED, prepare, 0)

    @pl.when(f < BLOCKS)
    def _():
        for k in range(ND - 1):
            p1_land(k).wait_recv()
        total = p1_dst[0].astype(f32)
        for part in range(1, ND):
            total += p1_dst[part].astype(f32)
        p2_buf[pl.ds(f, 1)] = total[None]
        for k in range(NF - 1):
            p2_copy(k).start()

    basis_forward(COLUMN)
    basis_forward(ACROSS_NEAR)
    lax.fori_loop(PREPARED, BATCH, prepare, 0)
    basis_forward(ACROSS_FAR)

    def unpack(half, goal_panel):
        for part in range(half * NZ, half * NZ + NZ):
            row = part * SIDE
            flat[row : row + SIDE, 0:128] = panels[part, 0:SIDE, :].astype(f32)
            tails = panels[part, 192:288, :].astype(f32)
            turned = pltpu.roll(tails, 64, 1)
            flat[row : row + 96, 128:192] = tails[:, 0:64]
            flat[row + 96 : row + SIDE, 128:192] = turned[0 : SIDE - 96, 0:64]
        low, high = half * NZ * SIDE, (half + 1) * NZ * SIDE
        for tap in range(9):
            tap_row, tap_col = tap // 3, tap % 3
            for begin, size, goal in (
                (0, 256, tap_row * 1024 + tap_col * 256),
                (256, 64, tap_row * 1024 + 768 + tap_col * 64),
            ):
                first = max(tap * CH + begin, low)
                last = min(tap * CH + begin + size, high)
                if first < last:
                    goal += first - tap * CH - begin
                    panel[goal_panel, goal : goal + last - first, :] = flat[first:last, :].astype(bf16)

    for half in range(NY):

        @pl.when(y == half)
        def _():
            unpack(half, 0)

    for k in range(NF - 1):
        sender, landing = p2_land(k)

        @pl.when(sender < BLOCKS)
        def _():
            landing.wait_recv()

    for part in range(BLOCKS):
        rows = p2_buf[part]
        high = rows.astype(bf16)
        m_stack[0:CS, part * 128 : (part + 1) * 128] = high
        m_stack[48 : 48 + CS, part * 128 : (part + 1) * 128] = (rows - high.astype(f32)).astype(bf16)
    main_rows = pl.ds(pl.multiple_of(y * (11 * 128), 128), 12 * 128)
    last_rows = pl.ds(pl.multiple_of((14 + 9 * y) * 128, 128), 128)
    both_v = jnp.dot(m_stack[:, : 12 * 128], panel[0, main_rows, :], preferred_element_type=f32) + jnp.dot(
        m_stack[:, 12 * 128 :], panel[0, last_rows, :], preferred_element_type=f32
    )
    part_v = both_v[0:CS] + both_v[48 : 48 + CS]
    tail_v = jnp.concatenate(
        [part_v[0:24, 128:192], jnp.concatenate([part_v[24:40, 128:192], jnp.zeros((8, 64), f32)], axis=0)],
        axis=1,
    )
    ag_buf[pl.ds(d, 1)] = jnp.concatenate([part_v[:, 0:128], tail_v], axis=0).astype(bf16)[None]
    for k in range(ND - 1):
        ag_copy(k).start()

    def half_product(b, half, which):
        line = pl.multiple_of(half * 128, 128)
        whole = jnp.dot(
            xl[b, pl.ds(line, POS), :],
            panel[which, pl.ds(pl.multiple_of(half * 2048, 2048), 1024), :],
            preferred_element_type=f32,
        )
        start = pl.multiple_of(half * 384, 128)
        whole += jnp.dot(
            xl[b, 64 : 64 + POS, pl.ds(start, 512)],
            panel[which, pl.ds(pl.multiple_of(1024 + half * 384, 128), 512), :],
            preferred_element_type=f32,
        )
        last = pl.multiple_of(768 + half * 128, 128)
        whole += jnp.dot(
            xl[b, 64 : 64 + POS, pl.ds(last, 128)],
            panel[which, pl.ds(pl.multiple_of(1792 + half * 128, 128), 128), :],
            preferred_element_type=f32,
        )
        return whole

    def first_half(b, carry):
        acc[b] = half_product(b, y, 0)
        return carry

    lax.fori_loop(0, BATCH, first_half, 0)

    for place in LANDS:
        basis_wait(place[0])
    for half in range(NY):

        @pl.when(y != half)
        def _():
            unpack(half, 1)

    def second_half(b, carry):
        proj = (acc[b] + half_product(b, 1 - y, 1)).astype(bf16)
        w_all[b] = jnp.dot(r_all[b], proj, preferred_element_type=f32)
        return carry

    lax.fori_loop(0, BATCH, second_half, 0)

    for k in range(ND - 1):
        ag_land(k).wait_recv()
    for part in range(NZ):
        both = ag_buf[part].astype(f32) + ag_buf[NZ + part].astype(f32)
        row = part * CS
        v_flat[row : row + CS, 0:128] = both[0:40]
        tails = both[40:64]
        turned = pltpu.roll(tails, 64, 1)
        half_line = lax.broadcasted_iota(jnp.int32, (24, 128), 1) < 64
        v_flat[row : row + 24, 128:256] = jnp.where(half_line, tails, 0.0)
        v_flat[row + 24 : row + CS, 128:256] = jnp.where(half_line, turned, 0.0)[0:16]
    v_full = v_flat[...]
    v_high = v_full.astype(bf16)
    v_low = (v_full - v_high.astype(f32)).astype(bf16)
    rotated = jnp.dot(bout_t[...], v_high, preferred_element_type=f32) + jnp.dot(
        bout_t[...], v_low, preferred_element_type=f32
    )
    q_pad[:, :SIDE] = rotated[:, :SIDE] * scale[...]
    q_full = q_pad[...]
    sums = []
    for b in range(BATCH):
        line = jnp.sum(w_all[b] * q_full, axis=0, keepdims=True)
        sums.append(line[:, :128] + line[:, 128:])
    ar_buf[pl.ds(f, 1)] = jnp.concatenate(sums, axis=0)[None]
    for k in range(NF - 1):
        ar_copy(k).start()

    proj_out[...] = q_pad[...].T[:SIDE, :]
    proj_store = pltpu.make_async_copy(proj_out, proj_hbm, load_sem.at[5])
    proj_store.start()
    phase = (time_ref[...].astype(f32) / 1000.0 + 0.008) / 1.008 * (math.pi / 2)
    weight = jnp.sin(phase) / math.sqrt(CH * CH * 9)
    for number in range(len(PLAN)):
        basis_copy(number).wait_send()

    @pl.when(f < BLOCKS)
    def _():
        for k in range(ND - 1):
            p1_copy(k).wait_send()
        for k in range(NF - 1):
            p2_copy(k).wait_send()

    for k in range(ND - 1):
        ag_copy(k).wait_send()

    for k in range(NF - 1):
        ar_land(k).wait_recv()
    total = ar_buf[0]
    for part in range(1, NF):
        total += ar_buf[part]
    score = jnp.broadcast_to(jnp.sum(total, axis=1, keepdims=True), (BATCH, 128))
    at = lax.broadcasted_iota(jnp.int32, (BATCH, 128), 0) == lax.broadcasted_iota(jnp.int32, (BATCH, 128), 1)
    score_ref[...] = jnp.sum(jnp.where(at, score, 0.0), axis=0, keepdims=True)[:, :BATCH] * weight
    proj_store.wait()
    for k in range(NF - 1):
        ar_copy(k).wait_send()


def on_device(x, cot, qx, qcot, timesteps, basis, bout, eig):
    hbm = pl.BlockSpec(memory_space=pl.ANY)
    vmem = pl.BlockSpec(memory_space=pltpu.VMEM)
    dma = pltpu.SemaphoreType.DMA
    raw, query_proj = pl.pallas_call(
        kernel,
        out_shape=(
            jax.ShapeDtypeStruct((1, BATCH), f32),
            jax.ShapeDtypeStruct((SIDE, CH), f32),
        ),
        in_specs=[hbm] * 7 + [vmem],
        out_specs=(vmem, hbm),
        scratch_shapes=[
            pltpu.VMEM((BATCH, 8, 64, CH), bf16),
            pltpu.VMEM((BATCH, 8, 64, CH), bf16),
            pltpu.VMEM((8, 64, CH), bf16),
            pltpu.VMEM((8, 64, CH), bf16),
            pltpu.VMEM((SIDE, SIDE), bf16),
            pltpu.VMEM((CH, CH), bf16),
            pltpu.VMEM((CH, CH), bf16),
            pltpu.VMEM((SIDE, CH), f32),
            pltpu.VMEM((CH, SIDE), f32),
            pltpu.VMEM((ND, PACK, 128), bf16),
            pltpu.VMEM((9 * CH, 256), f32),
            pltpu.VMEM((2, 3072, 256), bf16),
            pltpu.VMEM((BATCH + 1, 640, 1024), bf16),
            pltpu.VMEM((BATCH, CH, POS), bf16),
            pltpu.VMEM((BATCH, POS, 256), f32),
            pltpu.VMEM((BATCH, CH, 256), f32),
            pltpu.VMEM((SIDE, CH), f32),
            pltpu.VMEM((NY, CH, 128), f32),
            pltpu.VMEM((ND, CS, 128), bf16),
            pltpu.VMEM((ND, CS, 128), bf16),
            pltpu.VMEM((NF, CS, 128), f32),
            pltpu.VMEM((96, BLOCKS * 128), bf16),
            pltpu.VMEM((ND, 64, 128), bf16),
            pltpu.VMEM((CH, 256), f32),
            pltpu.VMEM((CH, 256), f32),
            pltpu.VMEM((NF, BATCH, 128), f32),
            dma((6,)),
            dma((BATCH,)),
            dma((BATCH,)),
            dma((len(PLAN),)),
            dma((len(PLAN),)),
            dma((ND,)),
            dma((ND,)),
            dma((NF,)),
            dma((NF,)),
            dma((ND,)),
            dma((ND,)),
            dma((NF,)),
            dma((NF,)),
        ],
        compiler_params=pltpu.CompilerParams(
            collective_id=0, has_side_effects=True, vmem_limit_bytes=58 * 1024 * 1024
        ),
        name="influence",
    )(x, cot, qx, qcot, basis, bout, eig.T, timesteps[None])
    return raw[0], query_proj.T


def solution(mesh):
    in_specs = (
        P("dp", None, None, None),
        P("dp", None, None, None),
        P("dp", None, None, None),
        P("dp", None, None, None),
        P("dp"),
        P("dp", "factor"),
        P(),
        P(None, "factor"),
    )
    out_specs = (P("dp"), P(None, "factor"))
    return jax.shard_map(
        on_device, mesh=mesh, in_specs=in_specs, out_specs=out_specs, check_vma=False
    )
```

time: 238 us -> 55.6 us (0.23); the launches traced: 235 us -> 55.5 us
  blocking collectives: 95.1 us -> 0 us
  local copies, waits for them, and re-layouts: 75.3 us -> 2.87 us
  Pallas kernels: 0 us -> 52 us
  matrix products: 34.2 us -> 0 us
  waiting for transfers between devices: 15.3 us -> 0 us
  between operations: 14.1 us -> 0.64 us
    all_gather x1 -> x0, blocking collectives: 52.8 us -> none  [on_device(): piece = lax.all_gather(input_basis, 'dp', axis=0, tiled=True)]
    pallas_call x0 -> x1, Pallas kernels: none -> 52 us  [on_device(): pl.pallas_call(kernel, out_shape=(jax.ShapeDtypeStruct((1, BATCH), f32),...]
    concatenate x2 -> x0, local copies, waits for them, and re-layouts: 43.6 us -> none  [patch_matrix(): jnp.concatenate(taps, axis=-1)]
    psum x1 -> x0, blocking collectives: 42.3 us -> none  [on_device(): raw_scores = lax.psum(partial_scores, 'factor')]
    dot_general x7 -> x0, matrix products: 34.2 us -> none  [the longest x1 14.1 us: on_device(): jnp.dot(train_patches, piece, preferred_element_type=jnp.float32)]
    slice x2 -> x0, local copies, waits for them, and re-layouts: 25.1 us -> none  [patch_matrix(): padded[:, row_off:row_off + rows_count, col_off:col_off + cols_count, :]]
    psum x1 -> x0, waiting for transfers between devices: 15.3 us -> none  [on_device(): query_grad = lax.psum(partial_query, 'dp') / count]
    unnamed x20 -> x2, local copies, waits for them, and re-layouts: 6.49 us -> 2.87 us
  transfers between devices with their start and end apart: 1 -> 0, of which waited for: 1 -> 0; matrix products, arithmetic and copies ran while one was open for 35% -> 0% of each run, Pallas kernels for 0% -> 0%
where the time goes in v1:
time: 55.6 us; the launch traced here: 55.5 us
  Pallas kernels  52 us (94%)
  local copies, waits for them, and re-layouts  2.87 us (5%)
  between operations  0.64 us (1%)
    pallas_call x1, Pallas kernels, on_device(): pl.pallas_call(kernel, out_shape=(jax.ShapeDtypeStruct((1, BATCH), f32),...  52 us
    unnamed x2, local copies, waits for them, and re-layouts  2.87 us

profile of v1, /device:TPU:1, one launch (start us, length us, event | category | flops | bytes accessed | tf_op | source)
XLA Modules:
  0.0 55.5 jit_solution(9509042639230352728)
XLA Ops:
  0.6 52.0 %influence.1 = (f32[1,8]{1,0:T(1,128)}, f32[180,320]{1,0:T(8,128)}) custom-call(bf16[8,8,64,320]{3,2,1,0:T(8,128)(2,1)} %x_hbm.1, bf16[8,8,64,320]{3,2,1,0:T(8,128)(2,1)} %cot_hbm.1, bf16[1,8,64,320]{3,2,1,0:T(8,128)(2,1)} %qx_hbm.1, bf16[1,8,64,320]{3,2,1,0:T(8,128)(2,1)} %qcot_hbm.1, bf16[180,180]{1,0:T(8,128)(2,1)} %bin_hbm.1, bf16[320,320]{1,0:T(8,128)(2,1)} %bout_hbm.1, ...), custom_call_target="tpu_custom_call" | custom-call | tf_op jit(solution)/shard_map/influence/pallas_call | solution.py:442
  52.6 1.2 %copy.12 = f32[8]{0:T(128)} copy(f32[8]{0:T(128)} %bitcast.7) | data formatting | bytes 64
  53.8 1.7 %copy.13 = f32[320,180]{0,1:T(8,128)} copy(f32[320,180]{0,1:T(8,128)} %bitcast.5) | data formatting | bytes 460800

commit v2 on v1

--- a/solution.py
+++ b/solution.py
@@ -18,7 +18,8 @@
 CH = 320
 SIDE = 180
 CS = 40
-BLOCKS = 13
+BLOCKS = 12
+HALF = 1536
 POS = 512
 BATCH = 8
 PREPARED = 5
@@ -40,7 +41,7 @@
     ((0, -2), HALF_A, (0, 2)), ((0, 2), HALF_B, (0, -2)),
     ((0, -2), WHOLE, (0, 1)), ((0, 2), WHOLE, (0, -1)),
 ]
-ACROSS_NEAR = [((0, k), WHOLE, (1, 0)) for k in (1, -1, 2, -2)]
+ACROSS_NEAR = [((1, 0), WHOLE, (0, k)) for k in (1, -1)] + [((0, k), WHOLE, (1, 0)) for k in (2, -2)]
 ACROSS_FAR = [((0, k), WHOLE, (1, 0)) for k in (3, -3, 4)]
 PLAN = START + COLUMN + ACROSS_NEAR + ACROSS_FAR
 LANDS = {}
@@ -60,15 +61,12 @@
 )
 
 
-def block_of(y, part):
-    return jnp.where(part < BLOCKS - 1, part + 11 * y, 14 + 9 * y)
-
-
 def fill_patches(raw, xl, slot):
     x = raw.reshape(POS, CH).astype(f32)
     col = lax.broadcasted_iota(jnp.int32, (POS, 1), 0) % 64
-    main, rest = x[:, :256], x[:, 256:]
-    zero_rest = jnp.zeros((POS, 64), f32)
+    main = x[:, :256]
+    rest = jnp.concatenate([x[:, 256:], jnp.zeros((POS, 64), f32)], axis=1)
+    pad = jnp.zeros((POS, 32), f32)
 
     def left(v):
         return jnp.where(col == 0, 0.0, pltpu.roll(v, 1, 0))
@@ -76,21 +74,25 @@
     def right(v):
         return jnp.where(col == 63, 0.0, pltpu.roll(v, POS - 1, 0))
 
-    wide = jnp.concatenate([rest, zero_rest], axis=1)
-    swapped = pltpu.roll(wide, 64, 1)
     inside = pl.ds(64, POS)
     xl[slot, inside, 0:256] = left(main).astype(bf16)
-    xl[slot, inside, 256:512] = main.astype(bf16)
+    xl[slot, inside, 256:512] = jnp.concatenate([left(rest)[:, :64], x[:, 0:160], pad], axis=1).astype(bf16)
     xl[slot, inside, 512:768] = right(main).astype(bf16)
-    xl[slot, inside, 768:896] = (left(wide) + swapped).astype(bf16)
-    xl[slot, inside, 896:1024] = right(wide).astype(bf16)
+    xl[slot, inside, 768:1024] = jnp.concatenate([right(rest)[:, :64], x[:, 160:320], pad], axis=1).astype(bf16)
+
+
+LAYOUT = (
+    ((0, 256, 0), (256, 320, 256)),
+    ((0, 160, 320), (160, 320, 832)),
+    ((0, 256, 512), (256, 320, 768)),
+)
 
 
 def kernel(
     x_hbm, cot_hbm, qx_hbm, qcot_hbm, bin_hbm, bout_hbm, eig_hbm, time_ref,
     score_ref, proj_hbm,
     x_raw, cot_raw, qx_raw, qcot_raw, bin_raw, bout, bout_t, eig_raw, scale,
-    panels, flat, panel, xl, r_all, acc, w_all, proj_out,
+    panels, flat, panel, xl, r_all, acc, proj_all, w_all, proj_out,
     mq, p1_src, p1_dst, p2_buf, m_stack, ag_buf, v_flat, q_pad, ar_buf,
     load_sem, x_sem, cot_sem,
     bin_send, bin_recv, p1_send, p1_recv, p2_send, p2_recv, ag_send, ag_recv, ar_send, ar_recv,
@@ -135,22 +137,12 @@
     xl[BATCH, 0:64, :] = jnp.zeros((64, 1024), bf16)
     xl[BATCH, 576:640, :] = jnp.zeros((64, 1024), bf16)
 
-    bin_load.wait()
-    block = bin_raw[...].astype(f32)
-    tail_a = block[0:96, 128:180]
-    tail_b = jnp.concatenate([block[96:180, 128:180], jnp.zeros((12, 52), f32)], axis=0)
-    gap = jnp.zeros((96, 12), f32)
-    panels[pl.ds(d, 1), 0:192, :] = jnp.concatenate(
-        [block[:, 0:128], jnp.zeros((12, 128), f32)], axis=0
-    ).astype(bf16)[None]
-    panels[pl.ds(d, 1), 192:288, :] = jnp.concatenate([tail_a, gap, tail_b, gap], axis=1).astype(bf16)[None]
-
     qx_load.wait()
     qcot_load.wait()
     fill_patches(qx_raw[...], xl, BATCH)
     query_t = qcot_raw[...].reshape(POS, CH).T
     for half in range(NY):
-        number = block_of(half, jnp.minimum(f, BLOCKS - 1))
+        number = half * BLOCKS + jnp.minimum(f, BLOCKS - 1)
         mq[half] = jnp.dot(
             query_t,
             xl[
@@ -241,6 +233,16 @@
         for k in range(ND - 1):
             p1_copy(k).start()
 
+    bin_load.wait()
+    block = bin_raw[...].astype(f32)
+    tail_a = block[0:96, 128:180]
+    tail_b = jnp.concatenate([block[96:180, 128:180], jnp.zeros((12, 52), f32)], axis=0)
+    gap = jnp.zeros((96, 12), f32)
+    panels[pl.ds(d, 1), 0:192, :] = jnp.concatenate(
+        [block[:, 0:128], jnp.zeros((12, 128), f32)], axis=0
+    ).astype(bf16)[None]
+    panels[pl.ds(d, 1), 192:288, :] = jnp.concatenate([tail_a, gap, tail_b, gap], axis=1).astype(bf16)[None]
+
     for number in range(len(START)):
         basis_copy(number).start()
 
@@ -282,7 +284,7 @@
     lax.fori_loop(PREPARED, BATCH, prepare, 0)
     basis_forward(ACROSS_FAR)
 
-    def unpack(half, goal_panel):
+    def unpack(half):
         for part in range(half * NZ, half * NZ + NZ):
             row = part * SIDE
             flat[row : row + SIDE, 0:128] = panels[part, 0:SIDE, :].astype(f32)
@@ -293,21 +295,20 @@
         low, high = half * NZ * SIDE, (half + 1) * NZ * SIDE
         for tap in range(9):
             tap_row, tap_col = tap // 3, tap % 3
-            for begin, size, goal in (
-                (0, 256, tap_row * 1024 + tap_col * 256),
-                (256, 64, tap_row * 1024 + 768 + tap_col * 64),
-            ):
+            for begin, end, goal in LAYOUT[tap_col]:
                 first = max(tap * CH + begin, low)
-                last = min(tap * CH + begin + size, high)
+                last = min(tap * CH + end, high)
                 if first < last:
-                    goal += first - tap * CH - begin
-                    panel[goal_panel, goal : goal + last - first, :] = flat[first:last, :].astype(bf16)
-
+                    goal += tap_row * 1024 + first - tap * CH - begin
+                    panel[goal : goal + last - first, :] = flat[first:last, :].astype(bf16)
+
+    for k in range(1, NZ):
+        basis_wait((0, k))
     for half in range(NY):
 
         @pl.when(y == half)
         def _():
-            unpack(half, 0)
+            unpack(half)
 
     for k in range(NF - 1):
         sender, landing = p2_land(k)
@@ -321,11 +322,8 @@
         high = rows.astype(bf16)
         m_stack[0:CS, part * 128 : (part + 1) * 128] = high
         m_stack[48 : 48 + CS, part * 128 : (part + 1) * 128] = (rows - high.astype(f32)).astype(bf16)
-    main_rows = pl.ds(pl.multiple_of(y * (11 * 128), 128), 12 * 128)
-    last_rows = pl.ds(pl.multiple_of((14 + 9 * y) * 128, 128), 128)
-    both_v = jnp.dot(m_stack[:, : 12 * 128], panel[0, main_rows, :], preferred_element_type=f32) + jnp.dot(
-        m_stack[:, 12 * 128 :], panel[0, last_rows, :], preferred_element_type=f32
-    )
+    own_rows = pl.ds(pl.multiple_of(y * HALF, HALF), HALF)
+    both_v = jnp.dot(m_stack[...], panel[own_rows, :], preferred_element_type=f32)
     part_v = both_v[0:CS] + both_v[48 : 48 + CS]
     tail_v = jnp.concatenate(
         [part_v[0:24, 128:192], jnp.concatenate([part_v[24:40, 128:192], jnp.zeros((8, 64), f32)], axis=0)],
@@ -335,29 +333,20 @@
     for k in range(ND - 1):
         ag_copy(k).start()
 
-    def half_product(b, half, which):
-        line = pl.multiple_of(half * 128, 128)
-        whole = jnp.dot(
-            xl[b, pl.ds(line, POS), :],
-            panel[which, pl.ds(pl.multiple_of(half * 2048, 2048), 1024), :],
+    def half_product(b, half):
+        whole_row = jnp.dot(
+            xl[b, pl.ds(pl.multiple_of(half * 128, 128), POS), :],
+            panel[pl.ds(pl.multiple_of(half * 2048, 2048), 1024), :],
             preferred_element_type=f32,
         )
-        start = pl.multiple_of(half * 384, 128)
-        whole += jnp.dot(
-            xl[b, 64 : 64 + POS, pl.ds(start, 512)],
-            panel[which, pl.ds(pl.multiple_of(1024 + half * 384, 128), 512), :],
+        return whole_row + jnp.dot(
+            xl[b, 64 : 64 + POS, pl.ds(pl.multiple_of(half * 512, 512), 512)],
+            panel[pl.ds(pl.multiple_of(1024 + half * 512, 512), 512), :],
             preferred_element_type=f32,
         )
-        last = pl.multiple_of(768 + half * 128, 128)
-        whole += jnp.dot(
-            xl[b, 64 : 64 + POS, pl.ds(last, 128)],
-            panel[which, pl.ds(pl.multiple_of(1792 + half * 128, 128), 128), :],
-            preferred_element_type=f32,
-        )
-        return whole
 
     def first_half(b, carry):
-        acc[b] = half_product(b, y, 0)
+        acc[b] = half_product(b, y)
         return carry
 
     lax.fori_loop(0, BATCH, first_half, 0)
@@ -368,14 +357,19 @@
 
         @pl.when(y != half)
         def _():
-            unpack(half, 1)
+            unpack(half)
 
     def second_half(b, carry):
-        proj = (acc[b] + half_product(b, 1 - y, 1)).astype(bf16)
-        w_all[b] = jnp.dot(r_all[b], proj, preferred_element_type=f32)
+        proj_all[b] = (acc[b] + half_product(b, 1 - y)).astype(bf16)
         return carry
 
     lax.fori_loop(0, BATCH, second_half, 0)
+
+    def contract(b, carry):
+        w_all[b] = jnp.dot(r_all[b], proj_all[b], preferred_element_type=f32)
+        return carry
+
+    lax.fori_loop(0, BATCH, contract, 0, unroll=2)
 
     for k in range(ND - 1):
         ag_land(k).wait_recv()
@@ -435,6 +429,11 @@
         ar_copy(k).wait_send()
 
 
+def finish(raw_ref, proj_ref, score_ref, out_ref):
+    score_ref[...] = raw_ref[...]
+    out_ref[...] = proj_ref[...]
+
+
 def on_device(x, cot, qx, qcot, timesteps, basis, bout, eig):
     hbm = pl.BlockSpec(memory_space=pl.ANY)
     vmem = pl.BlockSpec(memory_space=pltpu.VMEM)
@@ -459,10 +458,11 @@
             pltpu.VMEM((CH, SIDE), f32),
             pltpu.VMEM((ND, PACK, 128), bf16),
             pltpu.VMEM((9 * CH, 256), f32),
-            pltpu.VMEM((2, 3072, 256), bf16),
+            pltpu.VMEM((2 * HALF, 256), bf16),
             pltpu.VMEM((BATCH + 1, 640, 1024), bf16),
             pltpu.VMEM((BATCH, CH, POS), bf16),
             pltpu.VMEM((BATCH, POS, 256), f32),
+            pltpu.VMEM((BATCH, POS, 256), bf16),
             pltpu.VMEM((BATCH, CH, 256), f32),
             pltpu.VMEM((SIDE, CH), f32),
             pltpu.VMEM((NY, CH, 128), f32),
@@ -493,7 +493,17 @@
         ),
         name="influence",
     )(x, cot, qx, qcot, basis, bout, eig.T, timesteps[None])
-    return raw[0], query_proj.T
+    scores, query_proj = pl.pallas_call(
+        finish,
+        out_shape=(
+            jax.ShapeDtypeStruct((1, BATCH), f32),
+            jax.ShapeDtypeStruct((SIDE, CH), f32),
+        ),
+        in_specs=[vmem, vmem],
+        out_specs=(vmem, vmem),
+        name="finish",
+    )(raw, query_proj)
+    return scores[0], query_proj.T
 
 
 def solution(mesh):

time: 55.6 us -> 49.2 us (0.88)
  Pallas kernels: 52 us -> 48.5 us
  local copies, waits for them, and re-layouts: 2.87 us -> 0 us
    pallas_call x1, Pallas kernels: 52 us -> 46.8 us  [on_device(): pl.pallas_call(kernel, out_shape=(jax.ShapeDtypeStruct((1, BATCH), f32),...]
    unnamed x2 -> x0, local copies, waits for them, and re-layouts: 2.87 us -> none
    pallas_call x0 -> x1, Pallas kernels: none -> 1.69 us  [on_device(): pl.pallas_call(finish, out_shape=(jax.ShapeDtypeStruct((1, BATCH), f32),...]
where the time goes in v2:
time: 49.2 us; the launch traced here: 49.1 us
  Pallas kernels  48.5 us (99%)
  between operations  0.64 us (1%)
    pallas_call x1, Pallas kernels, on_device(): pl.pallas_call(kernel, out_shape=(jax.ShapeDtypeStruct((1, BATCH), f32),...  46.8 us
    pallas_call x1, Pallas kernels, on_device(): pl.pallas_call(finish, out_shape=(jax.ShapeDtypeStruct((1, BATCH), f32),...  1.69 us

profile of v2, /device:TPU:1, one launch (start us, length us, event | category | flops | bytes accessed | tf_op | source)
XLA Modules:
  0.0 49.1 jit_solution(10578768749975885964)
XLA Ops:
  0.6 46.8 %influence.1 = (f32[1,8]{1,0:T(1,128)}, f32[180,320]{1,0:T(8,128)}) custom-call(bf16[8,8,64,320]{3,2,1,0:T(8,128)(2,1)} %x_hbm.1, bf16[8,8,64,320]{3,2,1,0:T(8,128)(2,1)} %cot_hbm.1, bf16[1,8,64,320]{3,2,1,0:T(8,128)(2,1)} %qx_hbm.1, bf16[1,8,64,320]{3,2,1,0:T(8,128)(2,1)} %qcot_hbm.1, bf16[180,180]{1,0:T(8,128)(2,1)} %bin_hbm.1, bf16[320,320]{1,0:T(8,128)(2,1)} %bout_hbm.1, ...), custom_call_target="tpu_custom_call" | custom-call | tf_op jit(solution)/shard_map/influence/pallas_call | solution.py:441
  47.4 1.7 %finish.1 = (f32[1,8]{1,0:T(1,128)}, f32[180,320]{1,0:T(8,128)}) custom-call(f32[1,8]{1,0:T(1,128)} %get-tuple-element.6.raw_ref, f32[180,320]{1,0:T(8,128)} %get-tuple-element.7.proj_ref), custom_call_target="tpu_custom_call" | custom-call | tf_op jit(solution)/shard_map/finish/pallas_call | solution.py:496
